TPU v7x, 32 devices: a whole 2x2x4 slice. The times are simulated.
32 devices in a mesh: groups: 2 (over y), basis: 4 (over z), dp: 2 (over x), sub: 2 (over core).
Axes of the slice: x: 2, y: 2, z: 4, core: 2. Of those that a mesh axis runs over, the one named last changes fastest.
Arguments:
- activations: bfloat16 [4096, 8192], P(('groups', 'dp'), 'basis'), parts along dimension 0, may hold values from -6 to 6
- gradients: bfloat16 [4096, 28672], P(('groups', 'dp'), 'basis'), parts along dimension 0, may hold values from -6 to 6
- act_basis: float32 [16384, 512], P(('groups', 'basis'), 'sub'), parts along dimension 0, may hold values from -0.09375 to 0.09375
- grad_basis: float32 [57344, 1024], P(('groups', 'basis'), 'sub'), parts along dimension 0, may hold values from -0.046875 to 0.046875
Outputs:
- moments: float32 [2048, 512], P(('groups', 'sub', 'basis'), 'dp'), parts along dimension 0
There are 2 independent parts, one for each index of `groups`. A program takes and returns all parts, laid end to end along the dimension named above; each array names one. Nothing has to cross between parts.
All inputs are finite; a program needn't handle non-finite values.
Results may differ from a plain program's by a relative error of at most 0.0003.
Values sent between devices are 32-bit elements; how exact they have to be, the bound alone decides.
A program may use at most 128 MiB of HBM per device.

v0:
```python
import jax
import jax.numpy as jnp
from jax import lax
from jax.sharding import PartitionSpec as P


def make_term(basis, rows_in):
    return lax.dot_general(
        basis,
        rows_in,
        (((0,), (1,)), ((), ())),
        precision=lax.Precision.HIGHEST,
        preferred_element_type=jnp.float32,
    )


def pair_products(left, right):
    return lax.dot_general(
        left,
        right,
        (((1,), (1,)), ((), ())),
        precision=lax.Precision.HIGHEST,
        preferred_element_type=jnp.float32,
    )


def body(activations, gradients, act_basis, grad_basis):
    act_rows = activations.astype(jnp.float32)
    grad_rows = gradients.astype(jnp.float32)
    ways = lax.axis_size("basis")
    place = lax.axis_index("basis")
    grad_count = grad_basis.shape[1]
    grad_mine = grad_count // ways
    full_act, full_grad = lax.psum(
        (make_term(act_basis, act_rows), make_term(grad_basis, grad_rows)), "basis"
    )
    own_grad = lax.dynamic_slice_in_dim(full_grad, place * grad_mine, grad_mine, 0)
    squared_act = full_act * full_act
    squared_grad = own_grad * own_grad
    partial_sums = pair_products(
        squared_grad, lax.all_gather(squared_act, "sub", axis=0, tiled=True)
    )
    summed = lax.psum_scatter(partial_sums, "dp", scatter_dimension=1, tiled=True)
    total_tokens = activations.shape[0] * lax.axis_size("dp")
    return summed / total_tokens


def solution(mesh):
    return jax.shard_map(
        body,
        mesh=mesh,
        in_specs=(
            P(("groups", "dp"), "basis"),
            P(("groups", "dp"), "basis"),
            P(("groups", "basis"), "sub"),
            P(("groups", "basis"), "sub"),
        ),
        out_specs=P(("groups", "sub", "basis"), "dp"),
        check_vma=False,
    )
```

profile of v0, /device:TPU:0, one launch (start us, length us, event | category | flops | bytes accessed | tf_op | source)
XLA Modules:
  0.0 231.4 jit_solution(3663414917324626465)
XLA Ops:
  6.5 0.0 copy-start
  6.5 0.0 all-reduce.3.cloned.1.call-start
  6.5 1.6 copy-done
  8.1 9.9 %fusion.5 = f32[256,1024]{1,0:T(8,128)} fusion(f32[2048,256]{1,0:T(8,128)S(1)} %copy-done, bf16[1024,2048]{1,0:T(8,128)(2,1)} %param.4), kind=kOutput, calls=%fused_computation.6 | convolution fusion | flops 6442450944 | bytes 7340032 | tf_op jit(solution)/shard_map/dot_general | solution.py:8
  18.0 50.8 %fusion.4 = f32[512,1024]{1,0:T(8,128)} fusion(f32[7168,512]{1,0:T(8,128)} %param.7, bf16[1024,7168]{1,0:T(8,128)(2,1)} %param.5), kind=kOutput, calls=%fused_computation.5 | convolution fusion | flops 45097156608 | bytes 31457280 | tf_op jit(solution)/shard_map/dot_general | solution.py:8
  68.8 0.0 all-reduce.3.cloned.1.call-update
  68.8 0.0 all-gather.2.cloned.1.call-start
  68.9 124.2 %all-reduce.3.cloned.1.call-done = (f32[256,1024]{1,0:T(8,128)}, f32[512,1024]{1,0:T(8,128)}) async-done(((f32[256,1024]{1,0:T(8,128)}, f32[512,1024]{1,0:T(8,128)}), (f32[256,1024]{1,0:T(8,128)}, f32[512,1024]{1,0:T(8,128)})) %all-reduce.3.cloned.1.call-update) | async-done | bytes 3145744 | tf_op jit(solution)/shard_map/psum | solution.py:34
  193.1 2.7 %mul.11 = f32[256,1024]{1,0:T(8,128)} multiply(f32[256,1024]{1,0:T(8,128)} %get-tuple-element.5, f32[256,1024]{1,0:T(8,128)} %get-tuple-element.5) | non-fusion elementwise | flops 262144 | bytes 3145728 | tf_op jit(solution)/shard_map/mul | solution.py:38
  195.8 0.0 all-gather.2.cloned.1.call-update
  195.8 0.0 reduce-scatter.2.cloned.1.call-start
  195.9 9.7 %all-gather.2.cloned.1.call-done = f32[512,1024]{1,0:T(8,128)} async-done(((f32[256,1024]{1,0:T(8,128)}), f32[512,1024]{1,0:T(8,128)}) %all-gather.2.cloned.1.call-update) | async-done | bytes 2097168 | tf_op jit(solution)/shard_map/all_gather | solution.py:41
  205.6 4.7 %fusion = f32[128,512]{1,0:T(8,128)} fusion(f32[512,1024]{1,0:T(8,128)} %all-gather.2.cloned.1.call-done, f32[512,1024]{1,0:T(8,128)} %get-tuple-element.6, s32[]{:T(128)S(6)} %select_n.3), kind=kOutput, calls=%fused_computation | convolution fusion | flops 805437440 | bytes 2883588 | tf_op jit(solution)/shard_map/dot_general | solution.py:18
  210.3 0.0 reduce-scatter.2.cloned.1.call-update
  210.3 13.0 %reduce-scatter.2.cloned.1.call-done = f32[128,256]{1,0:T(8,128)} async-done(((f32[128,512]{1,0:T(8,128)}), f32[128,256]{1,0:T(8,128)}) %reduce-scatter.2.cloned.1.call-update) | async-done | bytes 131088 | tf_op jit(solution)/shard_map/reduce_scatter | solution.py:43
  223.3 1.6 broadcast_multiply_fusion
Async XLA Ops:
  6.5 1.6 copy-start
  6.5 186.6 %all-reduce.3.cloned.1.call-start = ((), (), s32[]{:S(2)}) async-start(), calls=%async_computation.3 | async-start | bytes 6291456 | tf_op jit(solution)/shard_map/psum | solution.py:34
  68.8 136.8 %all-gather.2.cloned.1.call-start = ((), (), s32[]{:S(2)}) async-start(), calls=%async_computation.1 | async-start | bytes 3145728 | tf_op jit(solution)/shard_map/all_gather | solution.py:41
  195.8 27.4 %reduce-scatter.2.cloned.1.call-start = ((), (), s32[]{:S(2)}) async-start(), calls=%async_computation.2 | async-start | bytes 393216 | tf_op jit(solution)/shard_map/reduce_scatter | solution.py:43
Sparse Core Ops, SparseCore 0:
  69.0 124.0 all-reduce.2
  196.0 9.5 all-gather.1
  210.4 12.8 reduce-scatter.1
where the time goes:
time: 232 us; the launch traced here: 231 us
  waiting for transfers between devices  147 us (63%)
  matrix products  65.3 us (28%)
  between operations  13.1 us (6%)
  other arithmetic  4.3 us (2%)
    psum x1, waiting for transfers between devices, body(): lax.psum((make_term(act_basis, act_rows), make_term(grad_basis, grad_rows...  124 us
    dot_general x2, matrix products, make_term(): lax.dot_general(basis, rows_in, (((0,), (1,)), ((), ())), precision=lax.P...  60.7 us
    reduce_scatter x1, waiting for transfers between devices, body(): lax.psum_scatter(partial_sums, 'dp', scatter_dimension=1, tiled=True)  13 us
    all_gather x1, waiting for transfers between devices, body(): lax.all_gather(squared_act, 'sub', axis=0, tiled=True)  9.68 us
    dot_general x1, matrix products, pair_products(): lax.dot_general(left, right, (((1,), (1,)), ((), ())), precision=lax.Prec...  4.66 us
  transfers between devices with their start and end apart: 3, of which 3 were waited for; matrix products, arithmetic and copies ran while one was open for 0% of the time, Pallas kernels for 0%

commit v1 on v0

v1 whole, which is shorter than its diff:
```python
import jax
import jax.numpy as jnp
from jax import lax
from jax.sharding import PartitionSpec as P


def halves(basis):
    high = lax.reduce_precision(basis, 8, 7)
    return high.astype(jnp.bfloat16), (basis - high).astype(jnp.bfloat16)


def make_term(basis, rows_in):
    dims = (((0,), (1,)), ((), ()))
    high, low = halves(basis)
    return lax.dot_general(
        high, rows_in, dims, preferred_element_type=jnp.float32
    ) + lax.dot_general(low, rows_in, dims, preferred_element_type=jnp.float32)


def pair_products(left, right):
    return lax.dot_general(
        left,
        right,
        (((1,), (1,)), ((), ())),
        precision=lax.Precision.HIGHEST,
        preferred_element_type=jnp.float32,
    )


def body(activations, gradients, act_basis, grad_basis):
    full_act = lax.psum(make_term(act_basis, activations), "basis")
    own_grad = lax.psum_scatter(
        make_term(grad_basis, gradients), "basis", scatter_dimension=0, tiled=True
    )
    squared_act = lax.all_gather(full_act * full_act, "sub", axis=0, tiled=True)
    partial_sums = pair_products(own_grad * own_grad, squared_act)
    summed = lax.psum_scatter(partial_sums, "dp", scatter_dimension=1, tiled=True)
    return summed / (activations.shape[0] * lax.axis_size("dp"))


def solution(mesh):
    return jax.shard_map(
        body,
        mesh=mesh,
        in_specs=(
            P(("groups", "dp"), "basis"),
            P(("groups", "dp"), "basis"),
            P(("groups", "basis"), "sub"),
            P(("groups", "basis"), "sub"),
        ),
        out_specs=P(("groups", "sub", "basis"), "dp"),
        check_vma=False,
    )
```

time: 232 us -> 155 us (0.67)
  waiting for transfers between devices: 147 us -> 93.5 us
  matrix products: 65.3 us -> 43.5 us
    psum x1, waiting for transfers between devices: 124 us -> 39.3 us  [body(): full_act = lax.psum(make_term(act_basis, activations), 'basis')]
    reduce_scatter x0 -> x1, waiting for transfers between devices: none -> 43 us  [body(): lax.psum_scatter(make_term(grad_basis, gradients), 'basis', scatter_dimen...]
    dot_general x2 -> x4, matrix products: 60.7 us -> 38.9 us  [the longest x2 21.2 us: make_term(): lax.dot_general(high, rows_in, dims, preferred_element_type=jnp.float32)]
    all_gather x1, waiting for transfers between devices: 9.68 us -> 0.02 us  [body(): squared_act = lax.all_gather(full_act * full_act, 'sub', axis=0, tiled=True)]
  transfers between devices with their start and end apart: 3 -> 4, of which waited for: 3 -> 3; matrix products, arithmetic and copies ran while one was open for 0% -> 21% of each run, Pallas kernels for 0% -> 0%
where the time goes in v1:
time: 155 us
  waiting for transfers between devices  93.5 us (60%)
  matrix products  43.5 us (28%)
  between operations  13.2 us (9%)
  other arithmetic  4.29 us (3%)
    reduce_scatter x1, waiting for transfers between devices, body(): lax.psum_scatter(make_term(grad_basis, gradients), 'basis', scatter_dimen...  43 us
    psum x1, waiting for transfers between devices, body(): full_act = lax.psum(make_term(act_basis, activations), 'basis')  39.3 us
    dot_general x2, matrix products, make_term(): lax.dot_general(high, rows_in, dims, preferred_element_type=jnp.float32)  21.2 us
    dot_general x2, matrix products, make_term(): lax.dot_general(low, rows_in, dims, preferred_element_type=jnp.float32)  17.6 us
    reduce_scatter x1, waiting for transfers between devices, body(): lax.psum_scatter(partial_sums, 'dp', scatter_dimension=1, tiled=True)  11.2 us
    dot_general x1, matrix products, pair_products(): lax.dot_general(left, right, (((1,), (1,)), ((), ())), precision=lax.Prec...  4.66 us
  transfers between devices with their start and end apart: 4, of which 3 were waited for; matrix products, arithmetic and copies ran while one was open for 21% of the time, Pallas kernels for 0%

profile of v1, /device:TPU:0, one launch (start us, length us, event | category | flops | bytes accessed | tf_op | source)
XLA Modules:
  0.0 155.0 jit_solution(246806453590237030)
XLA Ops:
  6.5 0.0 copy-start.1
  6.5 0.0 all-reduce.2.cloned.1.call-start
  6.5 0.0 copy-start
  6.5 4.3 %fusion.7 = f32[256,1024]{1,0:T(8,128)S(1)} fusion(bf16[1024,2048]{1,0:T(8,128)(2,1)} %param.4, f32[2048,256]{1,0:T(8,128)} %param.6), kind=kOutput, calls=%fused_computation.10 | convolution fusion | flops 1074790400 | bytes 7340032 | tf_op jit(solution)/shard_map/dot_general | solution.py:15
  10.8 0.0 copy-done.1
  10.8 0.4 copy-done
  11.2 2.3 %convolution_add_fusion = f32[256,1024]{1,0:T(8,128)} fusion(f32[256,1024]{1,0:T(8,128)S(1)} %fusion.7, bf16[1024,2048]{1,0:T(8,128)(2,1)S(1)} %copy-done, f32[2048,256]{1,0:T(8,128)S(1)} %copy-done.1), kind=kOutput, calls=%fused_computation.9 | convolution fusion | flops 1075576832 | bytes 8388608 | tf_op jit(solution)/shard_map/dot_general | solution.py:17
  13.5 0.0 all-reduce.2.cloned.1.call-update
  13.5 0.0 all-gather.2.cloned.1.call-start
  13.6 15.3 %fusion.1 = f32[512,1024]{1,0:T(8,128)S(1)} fusion(bf16[1024,7168]{1,0:T(8,128)(2,1)} %param.5, f32[7168,512]{1,0:T(8,128)} %param.7), kind=kOutput, calls=%fused_computation.3 | convolution fusion | flops 7527202816 | bytes 31457280 | tf_op jit(solution)/shard_map/dot_general | solution.py:17
  28.9 39.3 %all-reduce.2.cloned.1.call-done = f32[256,1024]{1,0:T(8,128)} async-done(((f32[256,1024]{1,0:T(8,128)}), f32[256,1024]{1,0:T(8,128)}) %all-reduce.2.cloned.1.call-update) | async-done | bytes 1048592 | tf_op jit(solution)/shard_map/psum | solution.py:31
  68.2 2.7 %mul.7 = f32[256,1024]{1,0:T(8,128)} multiply(f32[256,1024]{1,0:T(8,128)} %all-reduce.2.cloned.1.call-done, f32[256,1024]{1,0:T(8,128)} %all-reduce.2.cloned.1.call-done) | non-fusion elementwise | flops 262144 | bytes 3145728 | tf_op jit(solution)/shard_map/mul | solution.py:35
  70.9 0.0 all-gather.2.cloned.1.call-update
  71.0 0.0 reduce-scatter.3.cloned.1.call-start
  71.0 17.0 %fusion.5 = f32[512,1024]{1,0:T(8,128)} fusion(f32[512,1024]{1,0:T(8,128)S(1)} %fusion.1, bf16[1024,7168]{1,0:T(8,128)(2,1)} %param.5, f32[7168,512]{1,0:T(8,128)} %param.7), kind=kOutput, calls=%fused_computation.8 | convolution fusion | flops 7524057088 | bytes 33554432 | tf_op jit(solution)/shard_map/dot_general | solution.py:15
  88.0 0.0 reduce-scatter.3.cloned.1.call-update
  88.0 0.0 reduce-scatter.5.cloned.1.call-start
  88.1 0.0 all-gather.2.cloned.1.call-done
  88.1 43.0 %reduce-scatter.3.cloned.1.call-done = f32[128,1024]{1,0:T(8,128)} async-done(((f32[512,1024]{1,0:T(8,128)}), f32[128,1024]{1,0:T(8,128)}) %reduce-scatter.3.cloned.1.call-update) | async-done | bytes 524304 | tf_op jit(solution)/shard_map/reduce_scatter | solution.py:32
  131.1 4.7 %fusion.8 = f32[128,512]{1,0:T(8,128)} fusion(f32[512,1024]{1,0:T(8,128)} %all-gather.2.cloned.1.call-done, f32[128,1024]{1,0:T(8,128)} %reduce-scatter.3.cloned.1.call-done), kind=kOutput, calls=%fused_computation.11 | convolution fusion | flops 805437440 | bytes 2883584 | tf_op jit(solution)/shard_map/dot_general | solution.py:21
  135.7 0.0 reduce-scatter.5.cloned.1.call-update
  135.8 11.2 %reduce-scatter.5.cloned.1.call-done = f32[128,256]{1,0:T(8,128)} async-done(((f32[128,512]{1,0:T(8,128)}), f32[128,256]{1,0:T(8,128)}) %reduce-scatter.5.cloned.1.call-update) | async-done | bytes 131088 | tf_op jit(solution)/shard_map/reduce_scatter | solution.py:37
  146.9 1.6 %broadcast_multiply_fusion = f32[128,256]{1,0:T(8,128)} fusion(f32[128,256]{1,0:T(8,128)} %reduce-scatter.5.cloned.1.call-done), kind=kLoop, calls=%fused_computation.13 | loop fusion | flops 32768 | bytes 262144 | tf_op jit(solution)/shard_map/div | solution.py:38
Async XLA Ops:
  6.5 4.3 %copy-start.1 = (f32[2048,256]{1,0:T(8,128)S(1)}, f32[2048,256]{1,0:T(8,128)}, u32[]{:S(2)}) copy-start(f32[2048,256]{1,0:T(8,128)} %param.6) | copy-start | bytes 6291460
  6.5 61.7 %all-reduce.2.cloned.1.call-start = ((), (), s32[]{:S(2)}) async-start(), calls=%async_computation.3 | async-start | bytes 2097152 | tf_op jit(solution)/shard_map/psum | solution.py:31
  6.5 4.7 %copy-start = (bf16[1024,2048]{1,0:T(8,128)(2,1)S(1)}, bf16[1024,2048]{1,0:T(8,128)(2,1)}, u32[]{:S(2)}) copy-start(bf16[1024,2048]{1,0:T(8,128)(2,1)} %param.4) | copy-start | bytes 12582916
  13.5 74.6 %all-gather.2.cloned.1.call-start = ((), (), s32[]{:S(2)}) async-start(), calls=%async_computation.4 | async-start | bytes 3145728 | tf_op jit(solution)/shard_map/all_gather | solution.py:35
  71.0 60.1 %reduce-scatter.3.cloned.1.call-start = ((), (), s32[]{:S(2)}) async-start(), calls=%async_computation.2 | async-start | bytes 2621440 | tf_op jit(solution)/shard_map/reduce_scatter | solution.py:32
  88.0 58.9 %reduce-scatter.5.cloned.1.call-start = ((), (), s32[]{:S(2)}) async-start(), calls=%async_computation.5 | async-start | bytes 393216 | tf_op jit(solution)/shard_map/reduce_scatter | solution.py:37
Sparse Core Ops, SparseCore 0:
  13.7 54.5 all-reduce.1
  71.1 9.9 all-gather.1
  88.2 42.8 reduce-scatter.2
  135.9 11.0 reduce-scatter.4

commit v2 on v1

--- a/solution.py
+++ b/solution.py
@@ -1,17 +1,376 @@
+import functools
+
 import jax
 import jax.numpy as jnp
 from jax import lax
+from jax.experimental import pallas as pl
+from jax.experimental.pallas import tpu as pltpu
 from jax.sharding import PartitionSpec as P
 
-
-def halves(basis):
+MESH = pl.DeviceIdType.MESH
+WAYS = 4
+EVECS = 128
+ROWS = 128
+STEPS = 4
+
+
+def chain_kernel(
+    total_tokens,
+    act_hbm,
+    grad_hbm,
+    act_basis_hbm,
+    grad_basis_hbm,
+    out_ref,
+    act,
+    grad,
+    act_basis,
+    grad_basis,
+    split,
+    acc,
+    part,
+    got,
+    squares,
+    x_out,
+    x_in,
+    sums,
+    final,
+    load_sem,
+    send_sem,
+    recv_sem,
+    pair_sem,
+    x_send,
+    x_recv,
+    final_send,
+    final_recv,
+):
+    z = lax.axis_index("basis")
+    d = lax.axis_index("dp")
+    s = lax.axis_index("sub")
+    tokens, features = act.shape
+    half = tokens // 2
+    act_blocks = act_basis.shape[1] // EVECS
+    grad_blocks = grad_basis.shape[0]
+    per_block = half // ROWS
+    chunks = part.shape[1]
+    act_chunks = act_blocks * per_block
+    piece = grad.shape[1] // STEPS
+    block_rows = (0, 3, 1, 2)
+
+    barrier = pltpu.get_barrier_semaphore()
+    for hop in range(1, WAYS):
+        pl.semaphore_signal(
+            barrier, inc=1, device_id={"basis": lax.rem(z + hop, WAYS)}, device_id_type=MESH
+        )
+    pl.semaphore_signal(barrier, inc=1, device_id={"dp": 1 - d}, device_id_type=MESH)
+    pl.semaphore_signal(barrier, inc=1, device_id={"sub": 1 - s}, device_id_type=MESH)
+
+    loads = [pltpu.make_async_copy(act_basis_hbm, act_basis, load_sem.at[0])]
+    for way in range(2):
+        rows = pl.ds(way * half, half)
+        loads.append(
+            pltpu.make_async_copy(act_hbm.at[rows, :], act.at[rows, :], load_sem.at[1 + way])
+        )
+    for way in range(2):
+        rows = pl.ds(way * half, half)
+        loads.append(
+            pltpu.make_async_copy(grad_hbm.at[rows, :], grad.at[rows, :], load_sem.at[3 + way])
+        )
+
+    def load_block(i):
+        column = block_rows[i] * EVECS
+        return pltpu.make_async_copy(
+            grad_basis_hbm.at[:, pl.ds(column, EVECS)], grad_basis.at[i], load_sem.at[5 + i]
+        )
+
+    for load in loads[:3]:
+        load.start()
+    load_block(0).start()
+    for load in loads[3:]:
+        load.start()
+    pl.semaphore_wait(barrier, WAYS + 1)
+
+    def hops(way):
+        return z if way else WAYS - 1 - z
+
+    def chunk_copy(way, c):
+        to = lax.rem(z + (1 if way else WAYS - 1), WAYS)
+        return pltpu.make_async_remote_copy(
+            src_ref=part.at[way, c],
+            dst_ref=got.at[way, c],
+            send_sem=send_sem.at[way, c],
+            recv_sem=recv_sem.at[way, c],
+            device_id={"basis": to},
+            device_id_type=MESH,
+        )
+
+    def serve(slot):
+        for way in range(2):
+            h = hops(way)
+            c = slot - (h - 1)
+
+            @pl.when((h >= 1) & (c >= 0) & (c < chunks))
+            def _():
+                copy = chunk_copy(way, c)
+                copy.wait_recv()
+                part[way, c] = part[way, c] + got[way, c]
+
+                @pl.when(h < WAYS - 1)
+                def _():
+                    copy.start()
+
+    def halves(basis):
+        high = basis.astype(jnp.bfloat16)
+        low = (basis - high.astype(jnp.float32)).astype(jnp.bfloat16)
+        return high, low
+
+    def product(rows_ref, way, first, size, basis, start, fresh):
+        where = pl.ds(first, size)
+        if basis is not None:
+            high, low = halves(basis[...])
+            split[where, pl.ds(0, EVECS)] = high
+            split[where, pl.ds(EVECS, EVECS)] = low
+        term = jnp.dot(
+            rows_ref[pl.ds(way * half, half), where],
+            split[where, :],
+            preferred_element_type=jnp.float32,
+        )
+        if fresh:
+            acc[...] = term
+        else:
+            acc[...] = acc[...] + term
+
+    def give(way, base):
+        value = acc[:, pl.ds(0, EVECS)] + acc[:, pl.ds(EVECS, EVECS)]
+        part[way, pl.ds(base, per_block)] = value.reshape(per_block, ROWS, EVECS)
+
+        @pl.when(hops(way) == 0)
+        def _():
+            for t in range(per_block):
+                chunk_copy(way, base + t).start()
+
+    loads[0].wait()
+    for e in range(act_blocks):
+        for way in range(2):
+            if e == 0:
+                loads[1 + way].wait()
+            basis = act_basis.at[:, pl.ds(e * EVECS, EVECS)] if way == 0 else None
+            product(act, way, 0, features, basis, 0, True)
+            give(way, e * per_block)
+    for i in range(1, grad_blocks):
+        load_block(i).start()
+
+    is_end = (z == 0) | (z == WAYS - 1)
+    side = z // (WAYS - 1)
+
+    def pair_copy():
+        return pltpu.make_async_remote_copy(
+            src_ref=squares.at[s],
+            dst_ref=squares.at[s],
+            send_sem=pair_sem.at[0],
+            recv_sem=pair_sem.at[1],
+            device_id={"sub": 1 - s},
+            device_id_type=MESH,
+        )
+
+    def square_act():
+        @pl.when(is_end)
+        def _():
+            for e in range(act_blocks):
+                value = part[side, pl.ds(e * per_block, per_block)]
+                squares[s, :, pl.ds(e * EVECS, EVECS)] = (value * value).reshape(half, EVECS)
+            pair_copy().start()
+
+    def x_copy(i):
+        return pltpu.make_async_remote_copy(
+            src_ref=x_out.at[i],
+            dst_ref=x_in.at[i],
+            send_sem=x_send.at[i],
+            recv_sem=x_recv.at[i],
+            device_id={"dp": 1 - d},
+            device_id_type=MESH,
+        )
+
+    def final_copy(i, row, from_side):
+        return pltpu.make_async_remote_copy(
+            src_ref=sums.at[i],
+            dst_ref=final.at[from_side],
+            send_sem=final_send.at[i],
+            recv_sem=final_recv.at[from_side],
+            device_id={"basis": row},
+            device_id_type=MESH,
+        )
+
+    def moments(i):
+        value = part[side, pl.ds(act_chunks + i * per_block, per_block)]
+        left = (value * value).reshape(half, EVECS).T
+
+        def pairs(which):
+            return jnp.dot(
+                left,
+                squares[which],
+                precision=lax.Precision.HIGHEST,
+                preferred_element_type=jnp.float32,
+            )
+
+        x_out[i] = pairs(1 - d)
+        x_copy(i).start()
+        sums[i] = pairs(d)
+
+    def hand_over(i, row):
+        x_copy(i).wait_recv()
+        sums[i] = sums[i] + x_in[i]
+
+        @pl.when(row != z)
+        def _():
+            final_copy(i, row, side).start()
+
+    def block(b, carry):
+        load_block_wait = pltpu.make_async_copy(
+            grad_basis_hbm.at[:, pl.ds(0, EVECS)], grad_basis.at[b], load_sem.at[5 + b]
+        )
+        load_block_wait.wait()
+        for way in range(2):
+
+            @pl.when(b == 0)
+            def _():
+                loads[3 + way].wait()
+
+            for step in range(STEPS):
+                k = way * STEPS + step
+                basis = grad_basis.at[b, pl.ds(step * piece, piece), :] if way == 0 else None
+                product(grad, way, step * piece, piece, basis, 0, step == 0)
+                if step == STEPS - 1:
+                    give(way, act_chunks + b * per_block)
+                if k % 2 == 1:
+                    serve(jnp.where(b == 0, k, act_chunks + (b - 1) * per_block + k // 2))
+                else:
+                    pl.when(b == 0)(functools.partial(serve, k))
+                if k == 3:
+                    pl.when(b == 1)(square_act)
+
+                    @pl.when((b >= 2) & is_end)
+                    def _():
+                        @pl.when(b == 2)
+                        def _():
+                            pair_copy().wait_recv()
+
+                        moments(b - 2)
+
+                if k == 7:
+
+                    @pl.when((b >= 2) & is_end)
+                    def _():
+                        hand_over(b - 2, (b - 2) * (WAYS - 1))
+
+        return carry
+
+    lax.fori_loop(0, grad_blocks, block, 0)
+
+    done = act_chunks + (grad_blocks - 1) * per_block
+    for slot in range(done, done + 2):
+        serve(slot)
+    pl.when(is_end)(lambda: moments(2))
+    for slot in range(done + 2, done + 6):
+        serve(slot)
+
+    @pl.when(is_end)
+    def _():
+        moments(3)
+        hand_over(2, block_rows[2])
+        hand_over(3, block_rows[3])
+
+    @pl.when(z != 0)
+    def _():
+        final_copy(0, z, 0).wait_recv()
+
+    @pl.when(z != WAYS - 1)
+    def _():
+        final_copy(0, z, 1).wait_recv()
+
+    @pl.when(z == 0)
+    def _():
+        out_ref[...] = (sums[0] + final[1]) / total_tokens
+
+    @pl.when(z == WAYS - 1)
+    def _():
+        out_ref[...] = (final[0] + sums[1]) / total_tokens
+
+    @pl.when(jnp.logical_not(is_end))
+    def _():
+        out_ref[...] = (final[0] + final[1]) / total_tokens
+
+    for way in range(2):
+
+        @pl.when(hops(way) < WAYS - 1)
+        def _():
+            def drain(c, carry):
+                chunk_copy(way, c).wait_send()
+                return carry
+
+            lax.fori_loop(0, chunks, drain, 0)
+
+    @pl.when(is_end)
+    def _():
+        pair_copy().wait_send()
+        for i in range(grad_blocks):
+            x_copy(i).wait_send()
+
+            @pl.when(z != block_rows[i])
+            def _():
+                final_copy(i, block_rows[i], side).wait_send()
+
+
+def chained(activations, gradients, act_basis, grad_basis):
+    tokens, act_features = activations.shape
+    grad_features = gradients.shape[1]
+    act_count, grad_count = act_basis.shape[1], grad_basis.shape[1]
+    half = tokens // 2
+    grad_blocks = grad_count // EVECS
+    chunks = (act_count + grad_count) // EVECS * (half // ROWS)
+    f32, bf16 = jnp.float32, jnp.bfloat16
+    dma = pltpu.SemaphoreType.DMA
+    return pl.pallas_call(
+        functools.partial(chain_kernel, tokens * lax.axis_size("dp")),
+        out_shape=jax.ShapeDtypeStruct((EVECS, act_count), f32),
+        in_specs=[pl.BlockSpec(memory_space=pl.ANY)] * 4,
+        out_specs=pl.BlockSpec(memory_space=pltpu.VMEM),
+        scratch_shapes=[
+            pltpu.VMEM((tokens, act_features), bf16),
+            pltpu.VMEM((tokens, grad_features), bf16),
+            pltpu.VMEM((act_features, act_count), f32),
+            pltpu.VMEM((grad_blocks, grad_features, EVECS), f32),
+            pltpu.VMEM((max(grad_features, act_features), 2 * EVECS), bf16),
+            pltpu.VMEM((half, 2 * EVECS), f32),
+            pltpu.VMEM((2, chunks, ROWS, EVECS), f32),
+            pltpu.VMEM((2, chunks, ROWS, EVECS), f32),
+            pltpu.VMEM((2, half, act_count), f32),
+            pltpu.VMEM((grad_blocks, EVECS, act_count), f32),
+            pltpu.VMEM((grad_blocks, EVECS, act_count), f32),
+            pltpu.VMEM((grad_blocks, EVECS, act_count), f32),
+            pltpu.VMEM((2, EVECS, act_count), f32),
+            dma((5 + grad_blocks,)),
+            dma((2, chunks)),
+            dma((2, chunks)),
+            dma((2,)),
+            dma((grad_blocks,)),
+            dma((grad_blocks,)),
+            dma((grad_blocks,)),
+            dma((2,)),
+        ],
+        compiler_params=pltpu.CompilerParams(
+            collective_id=0, has_side_effects=True, vmem_limit_bytes=60 * 1024 * 1024
+        ),
+    )(activations, gradients, act_basis, grad_basis)
+
+
+def split_basis(basis):
     high = lax.reduce_precision(basis, 8, 7)
     return high.astype(jnp.bfloat16), (basis - high).astype(jnp.bfloat16)
 
 
 def make_term(basis, rows_in):
     dims = (((0,), (1,)), ((), ()))
-    high, low = halves(basis)
+    high, low = split_basis(basis)
     return lax.dot_general(
         high, rows_in, dims, preferred_element_type=jnp.float32
     ) + lax.dot_general(low, rows_in, dims, preferred_element_type=jnp.float32)
@@ -39,8 +398,18 @@
 
 
 def solution(mesh):
+    sizes = mesh.shape
+    fits = sizes["basis"] == WAYS and sizes["dp"] == 2 and sizes["sub"] == 2
+
+    def per_device(activations, gradients, act_basis, grad_basis):
+        even = activations.shape[0] % (2 * ROWS) == 0
+        blocks = act_basis.shape[1] % EVECS == 0 and grad_basis.shape[1] == WAYS * EVECS
+        if fits and even and blocks:
+            return chained(activations, gradients, act_basis, grad_basis)
+        return body(activations, gradients, act_basis, grad_basis)
+
     return jax.shard_map(
-        body,
+        per_device,
         mesh=mesh,
         in_specs=(
             P(("groups", "dp"), "basis"),

time: 155 us -> 97.3 us (0.63); the launches traced: 155 us -> 95.3 us
  Pallas kernels: 0 us -> 93.8 us
  waiting for transfers between devices: 93.5 us -> 0 us
  matrix products: 43.5 us -> 0 us
  between operations: 13.2 us -> 0.01 us
  other arithmetic: 4.29 us -> 0 us
    pallas_call x0 -> x1, Pallas kernels: none -> 93.8 us  [chained(): pl.pallas_call(functools.partial(chain_kernel, tokens * lax.axis_size('dp...]
    reduce_scatter x2 -> x0, waiting for transfers between devices: 54.1 us -> none  [the longest x1 43 us: body(): lax.psum_scatter(make_term(grad_basis, gradients), 'basis', scatter_dimen...]
    dot_general x5 -> x0, matrix products: 43.5 us -> none  [the longest x2 21.2 us: make_term(): lax.dot_general(high, rows_in, dims, preferred_element_type=jnp.float32)]
    psum x1 -> x0, waiting for transfers between devices: 39.3 us -> none  [body(): full_act = lax.psum(make_term(act_basis, activations), 'basis')]
    mul x1 -> x0, other arithmetic: 2.72 us -> none  [body(): squared_act = lax.all_gather(full_act * full_act, 'sub', axis=0, tiled=True)]
    div x1 -> x0, other arithmetic: 1.57 us -> none  [body(): return summed / (activations.shape[0] * lax.axis_size('dp'))]
  transfers between devices with their start and end apart: 4 -> 0, of which waited for: 3 -> 0; matrix products, arithmetic and copies ran while one was open for 21% -> 0% of each run, Pallas kernels for 0% -> 0%
where the time goes in v2:
time: 97.3 us; the launch traced here: 95.3 us
  Pallas kernels  93.8 us (96%)
  local copies, waits for them, and re-layouts  1.57 us (2%)
    pallas_call x1, Pallas kernels, chained(): pl.pallas_call(functools.partial(chain_kernel, tokens * lax.axis_size('dp...  93.8 us

profile of v2, /device:TPU:0, one launch (start us, length us, event | category | flops | bytes accessed | tf_op | source)
XLA Modules:
  0.0 95.3 jit_solution(7914828384114689773)
XLA Ops:
  0.0 93.8 %shard_map.46 = f32[128,256]{1,0:T(8,128)} custom-call(bf16[1024,2048]{1,0:T(8,128)(2,1)} %act_hbm.1, bf16[1024,7168]{1,0:T(8,128)(2,1)} %grad_hbm.1, f32[2048,256]{1,0:T(8,128)} %act_basis_hbm.1, f32[7168,512]{1,0:T(8,128)} %grad_basis_hbm.1), custom_call_target="tpu_custom_call" | custom-call | tf_op jit(solution)/shard_map/pallas_call | solution.py:332
  93.8 1.6 %copy.6 = f32[128,256]{1,0:T(8,128)} copy(f32[128,256]{1,0:T(8,128)} %shard_map.46) | data formatting | bytes 262144

commit v3 on v2

--- a/solution.py
+++ b/solution.py
@@ -12,6 +12,7 @@
 EVECS = 128
 ROWS = 128
 STEPS = 4
+LAG = 2
 
 
 def chain_kernel(
@@ -106,7 +107,7 @@
     def serve(slot):
         for way in range(2):
             h = hops(way)
-            c = slot - (h - 1)
+            c = slot - LAG * (h - 1)
 
             @pl.when((h >= 1) & (c >= 0) & (c < chunks))
             def _():
@@ -204,12 +205,14 @@
         value = part[side, pl.ds(act_chunks + i * per_block, per_block)]
         left = (value * value).reshape(half, EVECS).T
 
+        left_high, left_low = halves(left)
+
         def pairs(which):
-            return jnp.dot(
-                left,
-                squares[which],
-                precision=lax.Precision.HIGHEST,
-                preferred_element_type=jnp.float32,
+            high, low = halves(squares[which])
+            return (
+                jnp.dot(left_high, high, preferred_element_type=jnp.float32)
+                + jnp.dot(left_high, low, preferred_element_type=jnp.float32)
+                + jnp.dot(left_low, high, preferred_element_type=jnp.float32)
             )
 
         x_out[i] = pairs(1 - d)
@@ -245,32 +248,31 @@
                     serve(jnp.where(b == 0, k, act_chunks + (b - 1) * per_block + k // 2))
                 else:
                     pl.when(b == 0)(functools.partial(serve, k))
-                if k == 3:
+                if k == 7:
                     pl.when(b == 1)(square_act)
 
-                    @pl.when((b >= 2) & is_end)
+                    @pl.when((b == 2) & is_end)
                     def _():
-                        @pl.when(b == 2)
-                        def _():
-                            pair_copy().wait_recv()
-
-                        moments(b - 2)
-
-                if k == 7:
-
-                    @pl.when((b >= 2) & is_end)
+                        pair_copy().wait_recv()
+                        moments(0)
+
+                    @pl.when((b == 3) & is_end)
                     def _():
-                        hand_over(b - 2, (b - 2) * (WAYS - 1))
+                        hand_over(0, block_rows[0])
+                        moments(1)
 
         return carry
 
     lax.fori_loop(0, grad_blocks, block, 0)
 
     done = act_chunks + (grad_blocks - 1) * per_block
-    for slot in range(done, done + 2):
+    for slot in range(done, done + LAG):
+        serve(slot)
+    pl.when(is_end)(lambda: hand_over(1, block_rows[1]))
+    for slot in range(done + LAG, done + 2 * LAG):
         serve(slot)
     pl.when(is_end)(lambda: moments(2))
-    for slot in range(done + 2, done + 6):
+    for slot in range(done + 2 * LAG, chunks + 2 * LAG):
         serve(slot)
 
     @pl.when(is_end)

time: 97.3 us -> 75.9 us (0.78); the launches traced: 95.3 us -> 75.3 us
  Pallas kernels: 93.8 us -> 73.7 us
    pallas_call x1, Pallas kernels: 93.8 us -> 73.7 us  [chained(): pl.pallas_call(functools.partial(chain_kernel, tokens * lax.axis_size('dp...]
where the time goes in v3:
time: 75.9 us; the launch traced here: 75.3 us
  Pallas kernels  73.7 us (97%)
  local copies, waits for them, and re-layouts  1.57 us (2%)
    pallas_call x1, Pallas kernels, chained(): pl.pallas_call(functools.partial(chain_kernel, tokens * lax.axis_size('dp...  73.7 us
    unnamed x1, local copies, waits for them, and re-layouts  1.57 us

profile of v3, /device:TPU:0, one launch (start us, length us, event | category | flops | bytes accessed | tf_op | source)
XLA Modules:
  0.0 75.3 jit_solution(17786986282595244063)
XLA Ops:
  0.0 73.7 %shard_map.46 = f32[128,256]{1,0:T(8,128)} custom-call(bf16[1024,2048]{1,0:T(8,128)(2,1)} %act_hbm.1, bf16[1024,7168]{1,0:T(8,128)(2,1)} %grad_hbm.1, f32[2048,256]{1,0:T(8,128)} %act_basis_hbm.1, f32[7168,512]{1,0:T(8,128)} %grad_basis_hbm.1), custom_call_target="tpu_custom_call" | custom-call | tf_op jit(solution)/shard_map/pallas_call | solution.py:334
  73.7 1.6 %copy.6 = f32[128,256]{1,0:T(8,128)} copy(f32[128,256]{1,0:T(8,128)} %shard_map.46) | data formatting | bytes 262144
